TPU v7x, 32 devices: a whole 2x2x4 slice. The times are simulated.
32 devices in a mesh: row: 4 (over z), col: 8 (over y, x, core).
Axes of the slice: x: 2, y: 2, z: 4, core: 2. Of those that a mesh axis runs over, the one named last changes fastest.
Arguments:
- layer_inputs: float32 [512, 16384], P(('row', 'col')), may hold values from -60 to 60
Outputs:
- gram: float32 [16384, 16384], P('row', 'col')
All inputs are finite; a program needn't handle non-finite values.
Results may differ from a plain program's by a relative error of at most 0.000073.
Values sent between devices are 32-bit elements; how exact they have to be, the bound alone decides.
A program may use at most 128 MiB of HBM per device.

v0:
```python
import jax
import jax.numpy as jnp
from jax import lax
from jax.sharding import PartitionSpec as P


def broadcast(block, axis, owner):
    block = jnp.where(lax.axis_index(axis) == owner, block, jnp.zeros_like(block))
    return lax.psum(block, axis)


def shards(layer_inputs):
    n_rows = lax.axis_size("row")
    n_cols = lax.axis_size("col")
    own_columns = lax.all_to_all(layer_inputs, "col", split_axis=1, concat_axis=0, tiled=True)
    whole_columns = lax.all_gather(own_columns, "row", axis=0, tiled=True)
    count_all = whole_columns.shape[0]
    factor = n_cols // n_rows
    row_index = lax.axis_index("row")
    pieces = []
    for offset in range(factor):
        pieces.append(broadcast(whole_columns, "col", row_index * factor + offset))
    row_panel = jnp.concatenate(pieces, axis=1)
    product = lax.dot_general(
        row_panel,
        whole_columns,
        (((0,), (0,)), ((), ())),
        precision=lax.Precision.HIGHEST,
        preferred_element_type=jnp.float32,
    )
    return product / count_all


def solution(mesh):
    placed = (P(("row", "col"), None),)
    return jax.shard_map(
        shards, mesh=mesh, in_specs=placed, out_specs=P("row", "col"), check_vma=False
    )
```

profile of v0, /device:TPU:3, one launch (start us, length us, event | category | flops | bytes accessed | tf_op | source)
XLA Modules:
  0.0 306.3 jit_solution(7262703732557688858)
XLA Ops:
  6.5 0.0 all-gather.2.cloned.1.call-start
  6.5 1.3 copy.6
  7.9 18.1 %all_to_all.19 = f32[16,8,2048]{2,0,1:T(8,128)} all-to-all(f32[16,8,2048]{2,0,1:T(8,128)S(1)} %bitcast.10), channel_id=1, replica_groups=mesh['row'=4,'col'=8] {'col'}, dimensions={1} | all-to-all | bytes 2097152 | tf_op jit(solution)/shard_map/all_to_all | solution.py:15
  26.0 0.0 all-gather.2.cloned.1.call-update
  26.0 0.0 all-reduce.3.cloned.1.call-start
  26.1 81.1 %all-gather.2.cloned.1.call-done = f32[512,2048]{1,0:T(8,128)} async-done(((f32[128,2048]{1,0:T(8,128)}), f32[512,2048]{1,0:T(8,128)}) %all-gather.2.cloned.1.call-update) | async-done | bytes 4194320 | tf_op jit(solution)/shard_map/all_gather | solution.py:16
  107.2 6.9 %broadcast_select_fusion.1 = (f32[512,2048]{1,0:T(8,128)}, f32[512,2048]{1,0:T(8,128)}) fusion(f32[512,2048]{1,0:T(8,128)} %all-gather.2.cloned.1.call-done, pred[]{:T(512)S(6)} %eq.6, pred[]{:T(512)S(6)} %eq.7), kind=kLoop, calls=%fused_computation.5 | loop fusion | flops 2097152 | bytes 12582914 | tf_op jit(solution)/shard_map/jit(_where)/select_n | solution.py:8
  114.0 0.0 all-reduce.3.cloned.1.call-update
  114.1 125.4 %all-reduce.3.cloned.1.call-done = (f32[512,2048]{1,0:T(8,128)}, f32[512,2048]{1,0:T(8,128)}) async-done(((f32[512,2048]{1,0:T(8,128)}, f32[512,2048]{1,0:T(8,128)}), (f32[512,2048]{1,0:T(8,128)}, f32[512,2048]{1,0:T(8,128)})) %all-reduce.3.cloned.1.call-update) | async-done | bytes 8388624 | tf_op jit(solution)/shard_map/psum | solution.py:9
  239.5 60.0 %convolution_multiply_fusion = f32[4096,2048]{1,0:T(8,128)} fusion(f32[512,2048]{1,0:T(8,128)} %all-gather.2.cloned.1.call-done, f32[512,2048]{1,0:T(8,128)} %get-tuple-element.5, f32[512,2048]{1,0:T(8,128)} %get-tuple-element.6), kind=kOutput, calls=%fused_computation | convolution fusion | flops 51550093312 | bytes 46137344 | tf_op jit(solution)/shard_map/dot_general | solution.py:24
Async XLA Ops:
  6.5 100.6 %all-gather.2.cloned.1.call-start = ((), (), s32[]{:S(2)}) async-start(), calls=%async_computation.1 | async-start | bytes 5242880 | tf_op jit(solution)/shard_map/all_gather | solution.py:16
  26.0 213.4 %all-reduce.3.cloned.1.call-start = ((), (), s32[]{:S(2)}) async-start(), calls=%async_computation.2 | async-start | bytes 16777216 | tf_op jit(solution)/shard_map/psum | solution.py:9
Sparse Core Ops, SparseCore 0:
  26.2 80.9 all-gather.1
  114.2 125.2 all-reduce.2
where the time goes:
time: 308 us; the launch traced here: 306 us
  waiting for transfers between devices  206 us (67%)
  matrix products  60 us (19%)
  blocking collectives  18.1 us (6%)
  between operations  13.4 us (4%)
  other arithmetic  6.89 us (2%)
    psum x1, waiting for transfers between devices, broadcast(): return lax.psum(block, axis)  125 us
    all_gather x1, waiting for transfers between devices, shards(): whole_columns = lax.all_gather(own_columns, 'row', axis=0, tiled=True)  81.1 us
    dot_general x1, matrix products, shards(): lax.dot_general(row_panel, whole_columns, (((0,), (0,)), ((), ())), preci...  60 us
    all_to_all x1, blocking collectives, shards(): lax.all_to_all(layer_inputs, 'col', split_axis=1, concat_axis=0, tiled=True)  18.1 us
    select_n x1, other arithmetic, broadcast(): jnp.where(lax.axis_index(axis) == owner, block, jnp.zeros_like(block))  6.89 us
  transfers between devices with their start and end apart: 2, of which 2 were waited for; matrix products, arithmetic and copies ran while one was open for 0% of the time, Pallas kernels for 0%

commit v1 on v0

v1 whole, which is shorter than its diff:
```python
import functools

import jax
import jax.numpy as jnp
from jax import lax
from jax.experimental import pallas as pl
from jax.experimental.pallas import tpu as pltpu
from jax.sharding import PartitionSpec as P

MESH = pl.DeviceIdType.MESH
CORES = 2


def bits_of(chips):
    return max(chips.bit_length() - 1, 0)


def chip_at(place, chips):
    total = 0
    for k in range(bits_of(chips)):
        total += 2**k * lax.rem(lax.div(place, 2**k) + lax.div(place, 2 ** (k + 1)), 2)
    return total


def place_of(chip, chips):
    total, above = 0, 0
    for k in reversed(range(bits_of(chips))):
        above = lax.rem(above + lax.rem(lax.div(chip, 2**k), 2), 2)
        total += 2**k * above
    return total


def gather_kernel(
    n_rows, n_cols, x_ref, own_ref, panel_ref,
    all_send, all_recv, up_send, down_send, chain_recv,
    ring_send, ring_recv, twin_send, twin_recv, local_sem,
):
    r, c = lax.axis_index("row"), lax.axis_index("col")
    chips = n_cols // CORES
    chip, core = lax.div(c, CORES), lax.rem(c, CORES)
    twin = c + 1 - 2 * core
    tok = x_ref.shape[0]
    width = own_ref.shape[1]
    half = width // 2
    rows = tok * CORES
    pieces = n_rows * chips
    place, root = place_of(chip, chips), place_of(r, chips)
    is_root = chip == r
    follow = CORES * chip_at(lax.rem(place + 1, chips), chips) + core
    before = CORES * chip_at(lax.rem(place + chips - 1, chips), chips) + core
    ring_to = (follow, before)
    hops = (
        lax.rem(place - root + chips, chips),
        lax.rem(root - place + chips, chips),
    )

    barrier = pltpu.get_barrier_semaphore()

    def greet(k, _):
        pl.semaphore_signal(
            barrier, inc=1, device_id=(r, lax.rem(c + k, n_cols)), device_id_type=MESH
        )
        return 0

    lax.fori_loop(1, n_cols, greet, 0)

    @pl.when(r > 0)
    def _():
        pl.semaphore_signal(barrier, inc=1, device_id=(r - 1, c), device_id_type=MESH)

    @pl.when(r < n_rows - 1)
    def _():
        pl.semaphore_signal(barrier, inc=1, device_id=(r + 1, c), device_id_type=MESH)

    above, below = (r > 0).astype(jnp.int32), (r < n_rows - 1).astype(jnp.int32)
    pl.semaphore_wait(barrier, n_cols - 1 + above + below)

    def token_rows(source):
        return pl.ds(pl.multiple_of((r * n_cols + source) * tok, tok), tok)

    def x_columns(block):
        return pl.ds(pl.multiple_of(block * width, width), width)

    def piece_rows(piece):
        return pl.ds(pl.multiple_of(piece * rows, rows), rows)

    def panel_columns(way, of_core):
        return pl.ds(pl.multiple_of(of_core * width + way * half, half), half)

    def all_copy(k):
        other = lax.rem(c + k, n_cols)
        return pltpu.make_async_remote_copy(
            src_ref=x_ref.at[:, x_columns(other)],
            dst_ref=own_ref.at[token_rows(c)],
            send_sem=all_send.at[other],
            recv_sem=all_recv.at[c],
            device_id=(r, other),
            device_id_type=MESH,
        )

    def chain_copy(piece, step):
        block = own_ref.at[piece_rows(piece)]
        return pltpu.make_async_remote_copy(
            src_ref=block,
            dst_ref=block,
            send_sem=(up_send if step > 0 else down_send).at[piece],
            recv_sem=chain_recv.at[piece],
            device_id=(r + step, c),
            device_id_type=MESH,
        )

    def panel_part(way, piece):
        return panel_ref.at[piece_rows(piece), panel_columns(way, core)]

    def ring_copy(way, piece, from_own):
        source = panel_part(way, piece)
        if from_own:
            source = own_ref.at[piece_rows(piece), pl.ds(way * half, half)]
        return pltpu.make_async_remote_copy(
            src_ref=source,
            dst_ref=panel_part(way, piece),
            send_sem=ring_send.at[way, piece],
            recv_sem=ring_recv.at[way, piece],
            device_id=(r, ring_to[way]),
            device_id_type=MESH,
        )

    def twin_copy(way, piece, from_own):
        source = panel_part(way, piece)
        if from_own:
            source = own_ref.at[piece_rows(piece), pl.ds(way * half, half)]
        return pltpu.make_async_remote_copy(
            src_ref=source,
            dst_ref=panel_part(way, piece),
            send_sem=twin_send.at[way, piece],
            recv_sem=twin_recv.at[way, piece],
            device_id=(r, twin),
            device_id_type=MESH,
        )

    def local_copy(piece):
        return pltpu.make_async_copy(
            own_ref.at[piece_rows(piece)],
            panel_ref.at[piece_rows(piece), pl.ds(pl.multiple_of(core * width, width), width)],
            local_sem.at[piece],
        )

    def own_columns():
        return pltpu.make_async_copy(
            x_ref.at[:, x_columns(c)], own_ref.at[token_rows(c)], all_recv.at[c]
        )

    own_columns().start()

    def send_all(k, _):
        all_copy(k).start()
        return 0

    lax.fori_loop(1, n_cols, send_all, 0)

    def from_root(piece):
        @pl.when(is_root)
        def _():
            for way in range(2):
                if chips > 1:
                    ring_copy(way, piece, True).start()
            for way in range(2):
                twin_copy(way, piece, True).start()
            local_copy(piece).start()

    def own_step(s):
        away, turn = lax.div(s, chips), lax.rem(s, chips)
        group = lax.rem(chip + turn, chips)

        @pl.when(away == 0)
        def _():
            for k in range(CORES):
                source = group * CORES + k
                block = own_ref.at[token_rows(source)]
                pltpu.make_async_copy(block, block, all_recv.at[source]).wait()
            piece = r * chips + group

            @pl.when(r > 0)
            def _():
                chain_copy(piece, -1).start()

            @pl.when(r < n_rows - 1)
            def _():
                chain_copy(piece, 1).start()

            from_root(piece)

        @pl.when(jnp.logical_and(away > 0, r - away >= 0))
        def _():
            piece = (r - away) * chips + group
            chain_copy(piece, 1).wait_recv()

            @pl.when(r < n_rows - 1)
            def _():
                chain_copy(piece, 1).start()

            from_root(piece)

        @pl.when(jnp.logical_and(away > 0, r + away < n_rows))
        def _():
            piece = (r + away) * chips + group
            chain_copy(piece, -1).wait_recv()

            @pl.when(r > 0)
            def _():
                chain_copy(piece, -1).start()

            from_root(piece)

    def pass_on(way, piece):
        ring_copy(way, piece, False).wait_recv()

        @pl.when(hops[way] < chips - 1)
        def _():
            ring_copy(way, piece, False).start()

        twin_copy(way, piece, False).start()

    def ring_step(way, s):
        away, turn = lax.div(s, chips), lax.rem(s, chips)
        group = lax.rem(r + turn, chips)

        @pl.when(r - away >= 0)
        def _():
            pass_on(way, (r - away) * chips + group)

        @pl.when(jnp.logical_and(away > 0, r + away < n_rows))
        def _():
            pass_on(way, (r + away) * chips + group)

    def step(s, _):
        @pl.when(s < pieces)
        def _():
            own_step(s)

        for way in range(2):
            late = s - hops[way]

            @pl.when(
                jnp.logical_and(
                    jnp.logical_not(is_root),
                    jnp.logical_and(late >= 0, late < pieces),
                )
            )
            def _():
                ring_step(way, late)

        return 0

    lax.fori_loop(0, pieces + chips - 1, step, 0)

    def finish_all(k, _):
        all_copy(k).wait_send()
        return 0

    lax.fori_loop(1, n_cols, finish_all, 0)

    def finish(piece, _):
        of_row = lax.div(piece, chips)

        @pl.when(jnp.logical_and(r < n_rows - 1, of_row <= r))
        def _():
            chain_copy(piece, 1).wait_send()

        @pl.when(jnp.logical_and(r > 0, of_row >= r))
        def _():
            chain_copy(piece, -1).wait_send()

        for way in range(2):
            if chips > 1:
                @pl.when(hops[way] < chips - 1)
                def _():
                    ring_copy(way, piece, False).wait_send()

            twin_copy(way, piece, False).wait_send()
            twin_copy(way, piece, False).wait_recv()

        @pl.when(is_root)
        def _():
            local_copy(piece).wait()

        return 0

    lax.fori_loop(0, pieces, finish, 0)


def gather(x, n_rows, n_cols):
    tok, features = x.shape
    width = features // n_cols
    total = tok * n_rows * n_cols
    chips = n_cols // CORES
    pieces = n_rows * chips
    dma = pltpu.SemaphoreType.DMA
    return pl.pallas_call(
        functools.partial(gather_kernel, n_rows, n_cols),
        out_shape=(
            jax.ShapeDtypeStruct((total, width), jnp.float32),
            jax.ShapeDtypeStruct((total, CORES * width), jnp.float32),
        ),
        in_specs=[pl.BlockSpec(memory_space=pl.ANY)],
        out_specs=(pl.BlockSpec(memory_space=pl.ANY),) * 2,
        scratch_shapes=[
            dma((n_cols,)), dma((n_cols,)),
            dma((pieces,)), dma((pieces,)), dma((pieces,)),
            dma((2, pieces)), dma((2, pieces)),
            dma((2, pieces)), dma((2, pieces)),
            dma((pieces,)),
        ],
        compiler_params=pltpu.CompilerParams(collective_id=0, has_side_effects=True),
        name="gather_columns",
    )(x)


def split(x):
    high = x.astype(jnp.bfloat16)
    low = (x - high.astype(jnp.float32)).astype(jnp.bfloat16)
    return high, low


def gram_kernel(scale, panel_ref, own_ref, out_ref, right):
    depth = own_ref.shape[0]

    @pl.when(pl.program_id(0) == 0)
    def _():
        high, low = split(own_ref[...])
        right[pl.ds(0, depth), :] = high
        right[pl.ds(depth, depth), :] = low
        right[pl.ds(2 * depth, depth), :] = high

    high, low = split(panel_ref[...].T)
    left = jnp.concatenate([high, high, low], axis=1)
    product = jnp.dot(left, right[...], preferred_element_type=jnp.float32)
    out_ref[...] = product * scale


def gram(own, panel, tile):
    depth, width = own.shape
    count = panel.shape[1]
    return pl.pallas_call(
        functools.partial(gram_kernel, 1.0 / depth),
        grid=(count // tile,),
        out_shape=jax.ShapeDtypeStruct((count, width), jnp.float32),
        in_specs=[
            pl.BlockSpec((depth, tile), lambda i: (0, i)),
            pl.BlockSpec((depth, width), lambda i: (0, 0), pipeline_mode=pl.Buffered(1)),
        ],
        out_specs=pl.BlockSpec((tile, width), lambda i: (i, 0)),
        scratch_shapes=[pltpu.VMEM((3 * depth, width), jnp.bfloat16)],
        compiler_params=pltpu.CompilerParams(vmem_limit_bytes=56 * 2**20),
        cost_estimate=pl.CostEstimate(
            flops=6 * depth * width * count,
            bytes_accessed=4 * (width * count + depth * (width + count)),
            transcendentals=0,
        ),
        name="gram_blocks",
    )(panel, own)


def shards(x):
    n_rows, n_cols = lax.axis_size("row"), lax.axis_size("col")
    own, panel = gather(x, n_rows, n_cols)
    depth = own.shape[0]
    if depth & (depth - 1):
        raise ValueError("token count")
    return gram(own, panel, 256)


def solution(mesh):
    if mesh.shape["col"] != CORES * mesh.shape["row"]:
        raise ValueError("mesh shape")
    placed = (P(("row", "col"), None),)
    return jax.shard_map(
        shards, mesh=mesh, in_specs=placed, out_specs=P("row", "col"), check_vma=False
    )
```

time: 308 us -> 173 us (0.56)
  the two profiles are of different devices: /device:TPU:3 before, /device:TPU:0 now
where the time goes in v1:
time: 173 us
  Pallas kernels  173 us (100%)
    pallas_call x1, Pallas kernels, gather(): pl.pallas_call(functools.partial(gather_kernel, n_rows, n_cols), out_shap...  139 us
    pallas_call x1, Pallas kernels, gram(): pl.pallas_call(functools.partial(gram_kernel, 1.0 / depth), grid=(count /...  34.1 us

profile of v1, /device:TPU:0, one launch (start us, length us, event | category | flops | bytes accessed | tf_op | source)
XLA Modules:
  0.0 173.1 jit_solution(14408210815250505244)
XLA Ops:
  0.0 139.0 %gather_columns.1 = (f32[512,2048]{1,0:T(8,128)}, f32[512,4096]{1,0:T(8,128)}) custom-call(f32[16,16384]{1,0:T(8,128)} %x_ref.1), custom_call_target="tpu_custom_call" | custom-call | tf_op jit(solution)/shard_map/gather_columns/pallas_call | solution.py:299
  139.0 34.1 %gram_blocks.1 = f32[4096,2048]{1,0:T(8,128)} custom-call(f32[512,4096]{1,0:T(8,128)} %get-tuple-element.7.panel_ref, f32[512,2048]{1,0:T(8,128)} %get-tuple-element.8.own_ref), custom_call_target="tpu_custom_call" | custom-call | flops 25769803776 | bytes 46137344 | tf_op jit(solution)/shard_map/gram_blocks/pallas_call | solution.py:344

commit v2 on v1

--- a/solution.py
+++ b/solution.py
@@ -9,6 +9,8 @@
 
 MESH = pl.DeviceIdType.MESH
 CORES = 2
+GROUPS = 8
+VMEM_LIMIT = 56 * 2**20
 
 
 def bits_of(chips):
@@ -31,7 +33,7 @@
 
 
 def gather_kernel(
-    n_rows, n_cols, x_ref, own_ref, panel_ref,
+    n_rows, n_cols, groups, x_ref, own_out, panel_out, own_ref, panel_ref,
     all_send, all_recv, up_send, down_send, chain_recv,
     ring_send, ring_recv, twin_send, twin_recv, local_sem,
 ):
@@ -42,8 +44,9 @@
     tok = x_ref.shape[0]
     width = own_ref.shape[1]
     half = width // 2
-    rows = tok * CORES
-    pieces = n_rows * chips
+    per = n_cols // groups
+    rows = tok * per
+    pieces = n_rows * groups
     place, root = place_of(chip, chips), place_of(r, chips)
     is_root = chip == r
     follow = CORES * chip_at(lax.rem(place + 1, chips), chips) + core
@@ -139,10 +142,21 @@
         )
 
     def local_copy(piece):
+        columns = pl.ds(pl.multiple_of(core * width, width), width)
+        panel_ref[piece_rows(piece), columns] = own_ref[piece_rows(piece), :]
+
+    def keep_own(piece):
         return pltpu.make_async_copy(
             own_ref.at[piece_rows(piece)],
-            panel_ref.at[piece_rows(piece), pl.ds(pl.multiple_of(core * width, width), width)],
-            local_sem.at[piece],
+            own_out.at[piece_rows(piece)],
+            local_sem.at[0, piece],
+        )
+
+    def keep_panel(piece):
+        return pltpu.make_async_copy(
+            panel_ref.at[piece_rows(piece)],
+            panel_out.at[piece_rows(piece)],
+            local_sem.at[1, piece],
         )
 
     def own_columns():
@@ -159,6 +173,8 @@
     lax.fori_loop(1, n_cols, send_all, 0)
 
     def from_root(piece):
+        keep_own(piece).start()
+
         @pl.when(is_root)
         def _():
             for way in range(2):
@@ -166,19 +182,19 @@
                     ring_copy(way, piece, True).start()
             for way in range(2):
                 twin_copy(way, piece, True).start()
-            local_copy(piece).start()
+            local_copy(piece)
 
     def own_step(s):
-        away, turn = lax.div(s, chips), lax.rem(s, chips)
-        group = lax.rem(chip + turn, chips)
+        away, turn = lax.div(s, groups), lax.rem(s, groups)
+        group = lax.rem(lax.div(CORES * chip, per) + turn, groups)
 
         @pl.when(away == 0)
         def _():
-            for k in range(CORES):
-                source = group * CORES + k
+            for k in range(per):
+                source = group * per + k
                 block = own_ref.at[token_rows(source)]
                 pltpu.make_async_copy(block, block, all_recv.at[source]).wait()
-            piece = r * chips + group
+            piece = r * groups + group
 
             @pl.when(r > 0)
             def _():
@@ -192,7 +208,7 @@
 
         @pl.when(jnp.logical_and(away > 0, r - away >= 0))
         def _():
-            piece = (r - away) * chips + group
+            piece = (r - away) * groups + group
             chain_copy(piece, 1).wait_recv()
 
             @pl.when(r < n_rows - 1)
@@ -203,7 +219,7 @@
 
         @pl.when(jnp.logical_and(away > 0, r + away < n_rows))
         def _():
-            piece = (r + away) * chips + group
+            piece = (r + away) * groups + group
             chain_copy(piece, -1).wait_recv()
 
             @pl.when(r > 0)
@@ -222,16 +238,16 @@
         twin_copy(way, piece, False).start()
 
     def ring_step(way, s):
-        away, turn = lax.div(s, chips), lax.rem(s, chips)
-        group = lax.rem(r + turn, chips)
+        away, turn = lax.div(s, groups), lax.rem(s, groups)
+        group = lax.rem(lax.div(CORES * r, per) + turn, groups)
 
         @pl.when(r - away >= 0)
         def _():
-            pass_on(way, (r - away) * chips + group)
+            pass_on(way, (r - away) * groups + group)
 
         @pl.when(jnp.logical_and(away > 0, r + away < n_rows))
         def _():
-            pass_on(way, (r + away) * chips + group)
+            pass_on(way, (r + away) * groups + group)
 
     def step(s, _):
         @pl.when(s < pieces)
@@ -261,7 +277,7 @@
     lax.fori_loop(1, n_cols, finish_all, 0)
 
     def finish(piece, _):
-        of_row = lax.div(piece, chips)
+        of_row = lax.div(piece, groups)
 
         @pl.when(jnp.logical_and(r < n_rows - 1, of_row <= r))
         def _():
@@ -280,24 +296,28 @@
             twin_copy(way, piece, False).wait_send()
             twin_copy(way, piece, False).wait_recv()
 
-        @pl.when(is_root)
-        def _():
-            local_copy(piece).wait()
-
+        keep_panel(piece).start()
         return 0
 
     lax.fori_loop(0, pieces, finish, 0)
+
+    def finish_kept(piece, _):
+        keep_own(piece).wait()
+        keep_panel(piece).wait()
+        return 0
+
+    lax.fori_loop(0, pieces, finish_kept, 0)
 
 
 def gather(x, n_rows, n_cols):
     tok, features = x.shape
     width = features // n_cols
     total = tok * n_rows * n_cols
-    chips = n_cols // CORES
-    pieces = n_rows * chips
+    groups = GROUPS if n_cols % GROUPS == 0 else n_cols
+    pieces = n_rows * groups
     dma = pltpu.SemaphoreType.DMA
     return pl.pallas_call(
-        functools.partial(gather_kernel, n_rows, n_cols),
+        functools.partial(gather_kernel, n_rows, n_cols, groups),
         out_shape=(
             jax.ShapeDtypeStruct((total, width), jnp.float32),
             jax.ShapeDtypeStruct((total, CORES * width), jnp.float32),
@@ -305,13 +325,17 @@
         in_specs=[pl.BlockSpec(memory_space=pl.ANY)],
         out_specs=(pl.BlockSpec(memory_space=pl.ANY),) * 2,
         scratch_shapes=[
+            pltpu.VMEM((total, width), jnp.float32),
+            pltpu.VMEM((total, CORES * width), jnp.float32),
             dma((n_cols,)), dma((n_cols,)),
             dma((pieces,)), dma((pieces,)), dma((pieces,)),
             dma((2, pieces)), dma((2, pieces)),
             dma((2, pieces)), dma((2, pieces)),
-            dma((pieces,)),
+            dma((2, pieces)),
         ],
-        compiler_params=pltpu.CompilerParams(collective_id=0, has_side_effects=True),
+        compiler_params=pltpu.CompilerParams(
+            collective_id=0, has_side_effects=True, vmem_limit_bytes=VMEM_LIMIT
+        ),
         name="gather_columns",
     )(x)
 
@@ -351,7 +375,7 @@
         ],
         out_specs=pl.BlockSpec((tile, width), lambda i: (i, 0)),
         scratch_shapes=[pltpu.VMEM((3 * depth, width), jnp.bfloat16)],
-        compiler_params=pltpu.CompilerParams(vmem_limit_bytes=56 * 2**20),
+        compiler_params=pltpu.CompilerParams(vmem_limit_bytes=VMEM_LIMIT),
         cost_estimate=pl.CostEstimate(
             flops=6 * depth * width * count,
             bytes_accessed=4 * (width * count + depth * (width + count)),
@@ -367,7 +391,7 @@
     depth = own.shape[0]
     if depth & (depth - 1):
         raise ValueError("token count")
-    return gram(own, panel, 256)
+    return gram(own, panel, 512)
 
 
 def solution(mesh):

time: 173 us -> 150 us (0.87)
  the two profiles are of different devices: /device:TPU:0 before, /device:TPU:3 now
where the time goes in v2:
time: 150 us; the launch traced here: 149 us
  Pallas kernels  149 us (99%)
    pallas_call x1, Pallas kernels, gather(): pl.pallas_call(functools.partial(gather_kernel, n_rows, n_cols, groups),...  116 us
    pallas_call x1, Pallas kernels, gram(): pl.pallas_call(functools.partial(gram_kernel, 1.0 / depth), grid=(count /...  33 us

profile of v2, /device:TPU:3, one launch (start us, length us, event | category | flops | bytes accessed | tf_op | source)
XLA Modules:
  0.0 148.9 jit_solution(1942994380923703184)
XLA Ops:
  0.0 115.9 %gather_columns.1 = (f32[512,2048]{1,0:T(8,128)}, f32[512,4096]{1,0:T(8,128)}) custom-call(f32[16,16384]{1,0:T(8,128)} %x_ref.1), custom_call_target="tpu_custom_call" | custom-call | tf_op jit(solution)/shard_map/gather_columns/pallas_call | solution.py:319
  115.9 33.0 %gram_blocks.1 = f32[4096,2048]{1,0:T(8,128)} custom-call(f32[512,4096]{1,0:T(8,128)} %get-tuple-element.7.panel_ref, f32[512,2048]{1,0:T(8,128)} %get-tuple-element.8.own_ref), custom_call_target="tpu_custom_call" | custom-call | flops 25769803776 | bytes 46137344 | tf_op jit(solution)/shard_map/gram_blocks/pallas_call | solution.py:368

commit v3 on v2

--- a/solution.py
+++ b/solution.py
@@ -10,6 +10,7 @@
 MESH = pl.DeviceIdType.MESH
 CORES = 2
 GROUPS = 8
+LAG = 2
 VMEM_LIMIT = 56 * 2**20
 
 
@@ -95,7 +96,7 @@
         return pltpu.make_async_remote_copy(
             src_ref=x_ref.at[:, x_columns(other)],
             dst_ref=own_ref.at[token_rows(c)],
-            send_sem=all_send.at[other],
+            send_sem=all_send,
             recv_sem=all_recv.at[c],
             device_id=(r, other),
             device_id_type=MESH,
@@ -106,7 +107,7 @@
         return pltpu.make_async_remote_copy(
             src_ref=block,
             dst_ref=block,
-            send_sem=(up_send if step > 0 else down_send).at[piece],
+            send_sem=(up_send if step > 0 else down_send).at[lax.div(piece, groups)],
             recv_sem=chain_recv.at[piece],
             device_id=(r + step, c),
             device_id_type=MESH,
@@ -122,7 +123,7 @@
         return pltpu.make_async_remote_copy(
             src_ref=source,
             dst_ref=panel_part(way, piece),
-            send_sem=ring_send.at[way, piece],
+            send_sem=ring_send.at[way],
             recv_sem=ring_recv.at[way, piece],
             device_id=(r, ring_to[way]),
             device_id_type=MESH,
@@ -135,8 +136,8 @@
         return pltpu.make_async_remote_copy(
             src_ref=source,
             dst_ref=panel_part(way, piece),
-            send_sem=twin_send.at[way, piece],
-            recv_sem=twin_recv.at[way, piece],
+            send_sem=twin_send,
+            recv_sem=twin_recv.at[piece],
             device_id=(r, twin),
             device_id_type=MESH,
         )
@@ -149,14 +150,14 @@
         return pltpu.make_async_copy(
             own_ref.at[piece_rows(piece)],
             own_out.at[piece_rows(piece)],
-            local_sem.at[0, piece],
+            local_sem.at[0],
         )
 
     def keep_panel(piece):
         return pltpu.make_async_copy(
             panel_ref.at[piece_rows(piece)],
             panel_out.at[piece_rows(piece)],
-            local_sem.at[1, piece],
+            local_sem.at[1],
         )
 
     def own_columns():
@@ -249,13 +250,31 @@
         def _():
             pass_on(way, (r + away) * groups + group)
 
+    def keep(piece):
+        columns = pl.ds(pl.multiple_of((1 - core) * width, width), width)
+        part = panel_ref.at[piece_rows(piece), columns]
+        pltpu.make_async_copy(part, part, twin_recv.at[piece]).wait()
+        keep_panel(piece).start()
+
+    def keep_step(s):
+        away, turn = lax.div(s, groups), lax.rem(s, groups)
+        group = lax.rem(lax.div(CORES * r, per) + turn, groups)
+
+        @pl.when(r - away >= 0)
+        def _():
+            keep((r - away) * groups + group)
+
+        @pl.when(jnp.logical_and(away > 0, r + away < n_rows))
+        def _():
+            keep((r + away) * groups + group)
+
     def step(s, _):
         @pl.when(s < pieces)
         def _():
             own_step(s)
 
         for way in range(2):
-            late = s - hops[way]
+            late = s - LAG * hops[way]
 
             @pl.when(
                 jnp.logical_and(
@@ -266,47 +285,39 @@
             def _():
                 ring_step(way, late)
 
+        last = s - LAG * chips
+
+        @pl.when(last >= 0)
+        def _():
+            keep_step(last)
+
         return 0
 
-    lax.fori_loop(0, pieces + chips - 1, step, 0)
-
-    def finish_all(k, _):
-        all_copy(k).wait_send()
-        return 0
-
-    lax.fori_loop(1, n_cols, finish_all, 0)
-
-    def finish(piece, _):
-        of_row = lax.div(piece, groups)
-
-        @pl.when(jnp.logical_and(r < n_rows - 1, of_row <= r))
-        def _():
-            chain_copy(piece, 1).wait_send()
-
-        @pl.when(jnp.logical_and(r > 0, of_row >= r))
-        def _():
-            chain_copy(piece, -1).wait_send()
-
-        for way in range(2):
-            if chips > 1:
-                @pl.when(hops[way] < chips - 1)
-                def _():
-                    ring_copy(way, piece, False).wait_send()
-
-            twin_copy(way, piece, False).wait_send()
-            twin_copy(way, piece, False).wait_recv()
-
-        keep_panel(piece).start()
-        return 0
-
-    lax.fori_loop(0, pieces, finish, 0)
-
-    def finish_kept(piece, _):
-        keep_own(piece).wait()
-        keep_panel(piece).wait()
-        return 0
-
-    lax.fori_loop(0, pieces, finish_kept, 0)
+    lax.fori_loop(0, pieces + LAG * chips, step, 0)
+
+    def drain(ref, sem):
+        pltpu.make_async_copy(ref, ref, sem).wait()
+
+    drain(own_ref.at[pl.ds(0, (n_cols - 1) * tok)], all_send)
+    drain(own_ref, twin_send)
+    drain(own_ref, local_sem.at[0])
+    drain(panel_ref, local_sem.at[1])
+    for way in range(2):
+        if chips > 1:
+            @pl.when(hops[way] < chips - 1)
+            def _():
+                drain(own_ref.at[:, pl.ds(0, half)], ring_send.at[way])
+
+    for block in range(n_rows):
+        sent = own_ref.at[pl.ds(block * n_cols * tok, n_cols * tok)]
+
+        @pl.when(jnp.logical_and(r < n_rows - 1, block <= r))
+        def _():
+            drain(sent, up_send.at[block])
+
+        @pl.when(jnp.logical_and(r > 0, block >= r))
+        def _():
+            drain(sent, down_send.at[block])
 
 
 def gather(x, n_rows, n_cols):
@@ -327,11 +338,11 @@
         scratch_shapes=[
             pltpu.VMEM((total, width), jnp.float32),
             pltpu.VMEM((total, CORES * width), jnp.float32),
-            dma((n_cols,)), dma((n_cols,)),
-            dma((pieces,)), dma((pieces,)), dma((pieces,)),
-            dma((2, pieces)), dma((2, pieces)),
-            dma((2, pieces)), dma((2, pieces)),
-            dma((2, pieces)),
+            dma, dma((n_cols,)),
+            dma((n_rows,)), dma((n_rows,)), dma((pieces,)),
+            dma((2,)), dma((2, pieces)),
+            dma, dma((pieces,)),
+            dma((2,)),
         ],
         compiler_params=pltpu.CompilerParams(
             collective_id=0, has_side_effects=True, vmem_limit_bytes=VMEM_LIMIT

time: 150 us -> 125 us (0.83)
  Pallas kernels: 149 us -> 125 us
    pallas_call x1, Pallas kernels: 116 us -> 92.3 us  [gather(): pl.pallas_call(functools.partial(gather_kernel, n_rows, n_cols, groups),...]
where the time goes in v3:
time: 125 us
  Pallas kernels  125 us (100%)
    pallas_call x1, Pallas kernels, gather(): pl.pallas_call(functools.partial(gather_kernel, n_rows, n_cols, groups),...  92.3 us
    pallas_call x1, Pallas kernels, gram(): pl.pallas_call(functools.partial(gram_kernel, 1.0 / depth), grid=(count /...  33 us

profile of v3, /device:TPU:3, one launch (start us, length us, event | category | flops | bytes accessed | tf_op | source)
XLA Modules:
  0.0 125.3 jit_solution(1799316621442694692)
XLA Ops:
  0.0 92.3 %gather_columns.1 = (f32[512,2048]{1,0:T(8,128)}, f32[512,4096]{1,0:T(8,128)}) custom-call(f32[16,16384]{1,0:T(8,128)} %x_ref.1), custom_call_target="tpu_custom_call" | custom-call | tf_op jit(solution)/shard_map/gather_columns/pallas_call | solution.py:330
  92.3 33.0 %gram_blocks.1 = f32[4096,2048]{1,0:T(8,128)} custom-call(f32[512,4096]{1,0:T(8,128)} %get-tuple-element.7.panel_ref, f32[512,2048]{1,0:T(8,128)} %get-tuple-element.8.own_ref), custom_call_target="tpu_custom_call" | custom-call | flops 25769803776 | bytes 46137344 | tf_op jit(solution)/shard_map/gram_blocks/pallas_call | solution.py:379

commit v4 on v3

--- a/solution.py
+++ b/solution.py
@@ -11,6 +11,7 @@
 CORES = 2
 GROUPS = 8
 LAG = 2
+TILE = 512
 VMEM_LIMIT = 56 * 2**20
 
 
@@ -33,8 +34,15 @@
     return total
 
 
+def split(x):
+    high = x.astype(jnp.bfloat16)
+    low = (x - high.astype(jnp.float32)).astype(jnp.bfloat16)
+    return high, low
+
+
 def gather_kernel(
-    n_rows, n_cols, groups, x_ref, own_out, panel_out, own_ref, panel_ref,
+    n_rows, n_cols, groups, x_ref, own_out, panel_out, cross_out,
+    own_ref, panel_ref, right_ref, cross_ref, cross_sem,
     all_send, all_recv, up_send, down_send, chain_recv,
     ring_send, ring_recv, twin_send, twin_recv, local_sem,
 ):
@@ -268,6 +276,19 @@
         def _():
             keep((r + away) * groups + group)
 
+    tiles = panel_ref.shape[1] // TILE
+    early = n_rows // 2 * groups + LAG * chips
+    near_depth = own_ref.shape[0] // 2
+    near = pl.ds(pl.multiple_of(lax.div(r, n_rows // 2) * near_depth, near_depth), near_depth)
+
+    def cross_copy(tile):
+        slot = lax.rem(tile, 2)
+        return pltpu.make_async_copy(
+            cross_ref.at[slot],
+            cross_out.at[pl.ds(pl.multiple_of(tile * TILE, TILE), TILE)],
+            cross_sem.at[slot],
+        )
+
     def step(s, _):
         @pl.when(s < pieces)
         def _():
@@ -291,9 +312,34 @@
         def _():
             keep_step(last)
 
+        tile = s - early
+
+        @pl.when(tile == 0)
+        def _():
+            high, low = split(own_ref[near, :])
+            right_ref[pl.ds(0, near_depth), :] = low
+            right_ref[pl.ds(near_depth, near_depth), :] = high
+
+        @pl.when(jnp.logical_and(tile >= 0, tile < tiles))
+        def _():
+            slot = lax.rem(tile, 2)
+
+            @pl.when(tile >= 2)
+            def _():
+                cross_copy(tile - 2).wait()
+
+            columns = pl.ds(pl.multiple_of(tile * TILE, TILE), TILE)
+            high, low = split(panel_ref[near, columns].T)
+            left = jnp.concatenate([high, low], axis=1)
+            cross = jnp.dot(left, right_ref[...], preferred_element_type=jnp.float32)
+            cross_ref[slot] = cross.astype(jnp.bfloat16)
+            cross_copy(tile).start()
+
         return 0
 
-    lax.fori_loop(0, pieces + LAG * chips, step, 0)
+    lax.fori_loop(0, early + max(tiles, pieces + LAG * chips - early), step, 0)
+    for tile in range(max(tiles - 2, 0), tiles):
+        cross_copy(tile).wait()
 
     def drain(ref, sem):
         pltpu.make_async_copy(ref, ref, sem).wait()
@@ -332,12 +378,16 @@
         out_shape=(
             jax.ShapeDtypeStruct((total, width), jnp.float32),
             jax.ShapeDtypeStruct((total, CORES * width), jnp.float32),
+            jax.ShapeDtypeStruct((CORES * width, width), jnp.bfloat16),
         ),
         in_specs=[pl.BlockSpec(memory_space=pl.ANY)],
-        out_specs=(pl.BlockSpec(memory_space=pl.ANY),) * 2,
+        out_specs=(pl.BlockSpec(memory_space=pl.ANY),) * 3,
         scratch_shapes=[
             pltpu.VMEM((total, width), jnp.float32),
             pltpu.VMEM((total, CORES * width), jnp.float32),
+            pltpu.VMEM((total, width), jnp.bfloat16),
+            pltpu.VMEM((2, TILE, width), jnp.bfloat16),
+            dma((2,)),
             dma, dma((n_cols,)),
             dma((n_rows,)), dma((n_rows,)), dma((pieces,)),
             dma((2,)), dma((2, pieces)),
@@ -351,58 +401,56 @@
     )(x)
 
 
-def split(x):
-    high = x.astype(jnp.bfloat16)
-    low = (x - high.astype(jnp.float32)).astype(jnp.bfloat16)
-    return high, low
-
-
-def gram_kernel(scale, panel_ref, own_ref, out_ref, right):
+def gram_kernel(n_rows, scale, panel_ref, own_ref, cross_ref, out_ref, right):
     depth = own_ref.shape[0]
+    half = depth // 2
+    side = 1 - lax.div(lax.axis_index("row"), n_rows // 2)
+    far = pl.ds(pl.multiple_of(side * half, half), half)
 
     @pl.when(pl.program_id(0) == 0)
     def _():
-        high, low = split(own_ref[...])
-        right[pl.ds(0, depth), :] = high
-        right[pl.ds(depth, depth), :] = low
-        right[pl.ds(2 * depth, depth), :] = high
-
-    high, low = split(panel_ref[...].T)
-    left = jnp.concatenate([high, high, low], axis=1)
+        right[pl.ds(0, depth), :] = own_ref[...].astype(jnp.bfloat16)
+        high, low = split(own_ref[far, :])
+        right[pl.ds(depth, half), :] = low
+        right[pl.ds(depth + half, half), :] = high
+
+    high, low = split(panel_ref[far, :].T)
+    left = jnp.concatenate([panel_ref[...].T.astype(jnp.bfloat16), high, low], axis=1)
     product = jnp.dot(left, right[...], preferred_element_type=jnp.float32)
-    out_ref[...] = product * scale
-
-
-def gram(own, panel, tile):
+    out_ref[...] = (product + cross_ref[...].astype(jnp.float32)) * scale
+
+
+def gram(own, panel, cross, n_rows):
     depth, width = own.shape
     count = panel.shape[1]
     return pl.pallas_call(
-        functools.partial(gram_kernel, 1.0 / depth),
-        grid=(count // tile,),
+        functools.partial(gram_kernel, n_rows, 1.0 / depth),
+        grid=(count // TILE,),
         out_shape=jax.ShapeDtypeStruct((count, width), jnp.float32),
         in_specs=[
-            pl.BlockSpec((depth, tile), lambda i: (0, i)),
+            pl.BlockSpec((depth, TILE), lambda i: (0, i)),
             pl.BlockSpec((depth, width), lambda i: (0, 0), pipeline_mode=pl.Buffered(1)),
+            pl.BlockSpec((TILE, width), lambda i: (i, 0)),
         ],
-        out_specs=pl.BlockSpec((tile, width), lambda i: (i, 0)),
-        scratch_shapes=[pltpu.VMEM((3 * depth, width), jnp.bfloat16)],
+        out_specs=pl.BlockSpec((TILE, width), lambda i: (i, 0)),
+        scratch_shapes=[pltpu.VMEM((2 * depth, width), jnp.bfloat16)],
         compiler_params=pltpu.CompilerParams(vmem_limit_bytes=VMEM_LIMIT),
         cost_estimate=pl.CostEstimate(
-            flops=6 * depth * width * count,
-            bytes_accessed=4 * (width * count + depth * (width + count)),
+            flops=4 * depth * width * count,
+            bytes_accessed=4 * (width * count + depth * (width + count)) + 2 * width * count,
             transcendentals=0,
         ),
         name="gram_blocks",
-    )(panel, own)
+    )(panel, own, cross)
 
 
 def shards(x):
     n_rows, n_cols = lax.axis_size("row"), lax.axis_size("col")
-    own, panel = gather(x, n_rows, n_cols)
+    own, panel, cross = gather(x, n_rows, n_cols)
     depth = own.shape[0]
     if depth & (depth - 1):
         raise ValueError("token count")
-    return gram(own, panel, 512)
+    return gram(own, panel, cross, n_rows)
 
 
 def solution(mesh):

time: 125 us -> 121 us (0.968)
  Pallas kernels: 125 us -> 121 us
    pallas_call x1, Pallas kernels: 33 us -> 28.5 us  [gram(): pl.pallas_call(functools.partial(gram_kernel, n_rows, 1.0 / depth), grid=...]
where the time goes in v4:
time: 121 us
  Pallas kernels  121 us (100%)
    pallas_call x1, Pallas kernels, gather(): pl.pallas_call(functools.partial(gather_kernel, n_rows, n_cols, groups),...  92.3 us
    pallas_call x1, Pallas kernels, gram(): pl.pallas_call(functools.partial(gram_kernel, n_rows, 1.0 / depth), grid=...  28.5 us

profile of v4, /device:TPU:3, one launch (start us, length us, event | category | flops | bytes accessed | tf_op | source)
XLA Modules:
  0.0 120.8 jit_solution(4983487964420343487)
XLA Ops:
  0.0 92.3 %gather_columns.1 = (f32[512,2048]{1,0:T(8,128)}, f32[512,4096]{1,0:T(8,128)}, bf16[4096,2048]{1,0:T(8,128)(2,1)}) custom-call(f32[16,16384]{1,0:T(8,128)} %x_ref.1), custom_call_target="tpu_custom_call" | custom-call | tf_op jit(solution)/shard_map/gather_columns/pallas_call | solution.py:376
  92.3 28.5 %gram_blocks.1 = f32[4096,2048]{1,0:T(8,128)} custom-call(f32[512,4096]{1,0:T(8,128)} %get-tuple-element.8.panel_ref, f32[512,2048]{1,0:T(8,128)} %get-tuple-element.9.own_ref, bf16[4096,2048]{1,0:T(8,128)(2,1)} %get-tuple-element.10.cross_ref), custom_call_target="tpu_custom_call" | custom-call | flops 17179869184 | bytes 62914560 | tf_op jit(solution)/shard_map/gram_blocks/pallas_call | solution.py:426

commit v5 on v4

--- a/solution.py
+++ b/solution.py
@@ -41,8 +41,8 @@
 
 
 def gather_kernel(
-    n_rows, n_cols, groups, x_ref, own_out, panel_out, cross_out,
-    own_ref, panel_ref, right_ref, cross_ref, cross_sem,
+    n_rows, n_cols, groups, x_ref, own_out, panel_out, cross_out, near_out, left_out,
+    own_ref, panel_ref, right_ref, cross_ref, left_ref, cross_sem, left_sem, near_sem,
     all_send, all_recv, up_send, down_send, chain_recv,
     ring_send, ring_recv, twin_send, twin_recv, local_sem,
 ):
@@ -154,18 +154,34 @@
         columns = pl.ds(pl.multiple_of(core * width, width), width)
         panel_ref[piece_rows(piece), columns] = own_ref[piece_rows(piece), :]
 
+    near_depth = own_ref.shape[0] // 2
+    near_side = lax.div(r, n_rows // 2)
+    far_side = 1 - near_side
+    near = pl.ds(pl.multiple_of(near_side * near_depth, near_depth), near_depth)
+
+    def is_far(piece):
+        return lax.div(piece, pieces // 2) == far_side
+
+    def far_rows(piece):
+        return piece_rows(piece - far_side * (pieces // 2))
+
     def keep_own(piece):
         return pltpu.make_async_copy(
             own_ref.at[piece_rows(piece)],
-            own_out.at[piece_rows(piece)],
+            own_out.at[far_rows(piece)],
             local_sem.at[0],
         )
 
     def keep_panel(piece):
         return pltpu.make_async_copy(
             panel_ref.at[piece_rows(piece)],
-            panel_out.at[piece_rows(piece)],
+            panel_out.at[far_rows(piece)],
             local_sem.at[1],
+        )
+
+    def near_copy():
+        return pltpu.make_async_copy(
+            right_ref.at[pl.ds(near_depth, near_depth)], near_out, near_sem
         )
 
     def own_columns():
@@ -182,7 +198,9 @@
     lax.fori_loop(1, n_cols, send_all, 0)
 
     def from_root(piece):
-        keep_own(piece).start()
+        @pl.when(is_far(piece))
+        def _():
+            keep_own(piece).start()
 
         @pl.when(is_root)
         def _():
@@ -262,7 +280,10 @@
         columns = pl.ds(pl.multiple_of((1 - core) * width, width), width)
         part = panel_ref.at[piece_rows(piece), columns]
         pltpu.make_async_copy(part, part, twin_recv.at[piece]).wait()
-        keep_panel(piece).start()
+
+        @pl.when(is_far(piece))
+        def _():
+            keep_panel(piece).start()
 
     def keep_step(s):
         away, turn = lax.div(s, groups), lax.rem(s, groups)
@@ -278,8 +299,6 @@
 
     tiles = panel_ref.shape[1] // TILE
     early = n_rows // 2 * groups + LAG * chips
-    near_depth = own_ref.shape[0] // 2
-    near = pl.ds(pl.multiple_of(lax.div(r, n_rows // 2) * near_depth, near_depth), near_depth)
 
     def cross_copy(tile):
         slot = lax.rem(tile, 2)
@@ -287,6 +306,14 @@
             cross_ref.at[slot],
             cross_out.at[pl.ds(pl.multiple_of(tile * TILE, TILE), TILE)],
             cross_sem.at[slot],
+        )
+
+    def left_copy(tile):
+        slot = lax.rem(tile, 2)
+        return pltpu.make_async_copy(
+            left_ref.at[slot],
+            left_out.at[pl.ds(pl.multiple_of(tile * TILE, TILE), TILE)],
+            left_sem.at[slot],
         )
 
     def step(s, _):
@@ -319,6 +346,7 @@
             high, low = split(own_ref[near, :])
             right_ref[pl.ds(0, near_depth), :] = low
             right_ref[pl.ds(near_depth, near_depth), :] = high
+            near_copy().start()
 
         @pl.when(jnp.logical_and(tile >= 0, tile < tiles))
         def _():
@@ -327,9 +355,12 @@
             @pl.when(tile >= 2)
             def _():
                 cross_copy(tile - 2).wait()
+                left_copy(tile - 2).wait()
 
             columns = pl.ds(pl.multiple_of(tile * TILE, TILE), TILE)
             high, low = split(panel_ref[near, columns].T)
+            left_ref[slot] = high
+            left_copy(tile).start()
             left = jnp.concatenate([high, low], axis=1)
             cross = jnp.dot(left, right_ref[...], preferred_element_type=jnp.float32)
             cross_ref[slot] = cross.astype(jnp.bfloat16)
@@ -340,14 +371,16 @@
     lax.fori_loop(0, early + max(tiles, pieces + LAG * chips - early), step, 0)
     for tile in range(max(tiles - 2, 0), tiles):
         cross_copy(tile).wait()
+        left_copy(tile).wait()
+    near_copy().wait()
 
     def drain(ref, sem):
         pltpu.make_async_copy(ref, ref, sem).wait()
 
     drain(own_ref.at[pl.ds(0, (n_cols - 1) * tok)], all_send)
     drain(own_ref, twin_send)
-    drain(own_ref, local_sem.at[0])
-    drain(panel_ref, local_sem.at[1])
+    drain(own_ref.at[pl.ds(0, near_depth)], local_sem.at[0])
+    drain(panel_ref.at[pl.ds(0, near_depth)], local_sem.at[1])
     for way in range(2):
         if chips > 1:
             @pl.when(hops[way] < chips - 1)
@@ -376,18 +409,21 @@
     return pl.pallas_call(
         functools.partial(gather_kernel, n_rows, n_cols, groups),
         out_shape=(
-            jax.ShapeDtypeStruct((total, width), jnp.float32),
-            jax.ShapeDtypeStruct((total, CORES * width), jnp.float32),
+            jax.ShapeDtypeStruct((total // 2, width), jnp.float32),
+            jax.ShapeDtypeStruct((total // 2, CORES * width), jnp.float32),
             jax.ShapeDtypeStruct((CORES * width, width), jnp.bfloat16),
+            jax.ShapeDtypeStruct((total // 2, width), jnp.bfloat16),
+            jax.ShapeDtypeStruct((CORES * width, total // 2), jnp.bfloat16),
         ),
         in_specs=[pl.BlockSpec(memory_space=pl.ANY)],
-        out_specs=(pl.BlockSpec(memory_space=pl.ANY),) * 3,
+        out_specs=(pl.BlockSpec(memory_space=pl.ANY),) * 5,
         scratch_shapes=[
             pltpu.VMEM((total, width), jnp.float32),
             pltpu.VMEM((total, CORES * width), jnp.float32),
             pltpu.VMEM((total, width), jnp.bfloat16),
             pltpu.VMEM((2, TILE, width), jnp.bfloat16),
-            dma((2,)),
+            pltpu.VMEM((2, TILE, total // 2), jnp.bfloat16),
+            dma((2,)), dma((2,)), dma,
             dma, dma((n_cols,)),
             dma((n_rows,)), dma((n_rows,)), dma((pieces,)),
             dma((2,)), dma((2, pieces)),
@@ -401,56 +437,57 @@
     )(x)
 
 
-def gram_kernel(n_rows, scale, panel_ref, own_ref, cross_ref, out_ref, right):
-    depth = own_ref.shape[0]
-    half = depth // 2
-    side = 1 - lax.div(lax.axis_index("row"), n_rows // 2)
-    far = pl.ds(pl.multiple_of(side * half, half), half)
+def gram_kernel(scale, left_ref, panel_ref, near_ref, own_ref, cross_ref, out_ref, right):
+    half = own_ref.shape[0]
 
     @pl.when(pl.program_id(0) == 0)
     def _():
-        right[pl.ds(0, depth), :] = own_ref[...].astype(jnp.bfloat16)
-        high, low = split(own_ref[far, :])
-        right[pl.ds(depth, half), :] = low
-        right[pl.ds(depth + half, half), :] = high
-
-    high, low = split(panel_ref[far, :].T)
-    left = jnp.concatenate([panel_ref[...].T.astype(jnp.bfloat16), high, low], axis=1)
+        high, low = split(own_ref[...])
+        right[pl.ds(0, half), :] = near_ref[...]
+        right[pl.ds(half, half), :] = high
+        right[pl.ds(2 * half, half), :] = low
+        right[pl.ds(3 * half, half), :] = high
+
+    high, low = split(panel_ref[...].T)
+    left = jnp.concatenate([left_ref[...], high, high, low], axis=1)
     product = jnp.dot(left, right[...], preferred_element_type=jnp.float32)
     out_ref[...] = (product + cross_ref[...].astype(jnp.float32)) * scale
 
 
-def gram(own, panel, cross, n_rows):
-    depth, width = own.shape
+def gram(own, panel, cross, near, left):
+    half, width = own.shape
     count = panel.shape[1]
+    once = pl.Buffered(1)
     return pl.pallas_call(
-        functools.partial(gram_kernel, n_rows, 1.0 / depth),
+        functools.partial(gram_kernel, 0.5 / half),
         grid=(count // TILE,),
         out_shape=jax.ShapeDtypeStruct((count, width), jnp.float32),
         in_specs=[
-            pl.BlockSpec((depth, TILE), lambda i: (0, i)),
-            pl.BlockSpec((depth, width), lambda i: (0, 0), pipeline_mode=pl.Buffered(1)),
+            pl.BlockSpec((TILE, half), lambda i: (i, 0)),
+            pl.BlockSpec((half, TILE), lambda i: (0, i)),
+            pl.BlockSpec((half, width), lambda i: (0, 0), pipeline_mode=once),
+            pl.BlockSpec((half, width), lambda i: (0, 0), pipeline_mode=once),
             pl.BlockSpec((TILE, width), lambda i: (i, 0)),
         ],
         out_specs=pl.BlockSpec((TILE, width), lambda i: (i, 0)),
-        scratch_shapes=[pltpu.VMEM((2 * depth, width), jnp.bfloat16)],
+        scratch_shapes=[pltpu.VMEM((4 * half, width), jnp.bfloat16)],
         compiler_params=pltpu.CompilerParams(vmem_limit_bytes=VMEM_LIMIT),
         cost_estimate=pl.CostEstimate(
-            flops=4 * depth * width * count,
-            bytes_accessed=4 * (width * count + depth * (width + count)) + 2 * width * count,
+            flops=8 * half * width * count,
+            bytes_accessed=6 * (width * count + half * (width + count)),
             transcendentals=0,
         ),
         name="gram_blocks",
-    )(panel, own, cross)
+    )(left, panel, near, own, cross)
 
 
 def shards(x):
     n_rows, n_cols = lax.axis_size("row"), lax.axis_size("col")
-    own, panel, cross = gather(x, n_rows, n_cols)
-    depth = own.shape[0]
+    own, panel, cross, near, left = gather(x, n_rows, n_cols)
+    depth = 2 * own.shape[0]
     if depth & (depth - 1):
         raise ValueError("token count")
-    return gram(own, panel, cross, n_rows)
+    return gram(own, panel, cross, near, left)
 
 
 def solution(mesh):

time: 121 us -> 120 us (level)
  no operation moved by 1% of the time
where the time goes in v5:
time: 120 us
  Pallas kernels  120 us (100%)
    pallas_call x1, Pallas kernels, gather(): pl.pallas_call(functools.partial(gather_kernel, n_rows, n_cols, groups),...  92.3 us
    pallas_call x1, Pallas kernels, gram(): pl.pallas_call(functools.partial(gram_kernel, 0.5 / half), grid=(count //...  27.7 us

profile of v5, /device:TPU:3, one launch (start us, length us, event | category | flops | bytes accessed | tf_op | source)
XLA Modules:
  0.0 119.9 jit_solution(9748892207364874412)
XLA Ops:
  0.0 92.3 %gather_columns.1 = (f32[256,2048]{1,0:T(8,128)}, f32[256,4096]{1,0:T(8,128)}, bf16[4096,2048]{1,0:T(8,128)(2,1)}, bf16[256,2048]{1,0:T(8,128)(2,1)}, bf16[4096,256]{1,0:T(8,128)(2,1)}) custom-call(f32[16,16384]{1,0:T(8,128)} %x_ref.1), custom_call_target="tpu_custom_call" | custom-call | tf_op jit(solution)/shard_map/gather_columns/pallas_call | solution.py:409
  92.3 27.7 %gram_blocks.1 = f32[4096,2048]{1,0:T(8,128)} custom-call(bf16[4096,256]{1,0:T(8,128)(2,1)} %get-tuple-element.10.left_ref, f32[256,4096]{1,0:T(8,128)} %get-tuple-element.11.panel_ref, bf16[256,2048]{1,0:T(8,128)(2,1)} %get-tuple-element.12.near_ref, f32[256,2048]{1,0:T(8,128)} %get-tuple-element.13.own_ref, bf16[4096,2048]{1,0:T(8,128)(2,1)} %get-tuple-element.14.cross_ref), custom_call_target="tpu_custom_call" | custom-call | flops 17179869184 | bytes 59768832 | tf_op jit(solution)/shard_map/gram_blocks/pallas_call | solution.py:461

commit v6 on v5

--- a/solution.py
+++ b/solution.py
@@ -450,8 +450,10 @@
 
     high, low = split(panel_ref[...].T)
     left = jnp.concatenate([left_ref[...], high, high, low], axis=1)
-    product = jnp.dot(left, right[...], preferred_element_type=jnp.float32)
-    out_ref[...] = (product + cross_ref[...].astype(jnp.float32)) * scale
+    for start in range(0, out_ref.shape[1], TILE):
+        part = pl.ds(start, TILE)
+        product = jnp.dot(left, right[:, part], preferred_element_type=jnp.float32)
+        out_ref[:, part] = (product + cross_ref[:, part].astype(jnp.float32)) * scale
 
 
 def gram(own, panel, cross, near, left):

time: 120 us -> 120 us (level)
  no operation moved by 1% of the time
where the time goes in v6:
time: 120 us
  Pallas kernels  120 us (100%)
    pallas_call x1, Pallas kernels, gather(): pl.pallas_call(functools.partial(gather_kernel, n_rows, n_cols, groups),...  92.3 us
    pallas_call x1, Pallas kernels, gram(): pl.pallas_call(functools.partial(gram_kernel, 0.5 / half), grid=(count //...  27.7 us

profile of v6, /device:TPU:3, one launch (start us, length us, event | category | flops | bytes accessed | tf_op | source)
XLA Modules:
  0.0 119.9 jit_solution(9748892207364874412)
XLA Ops:
  0.0 92.3 %gather_columns.1 = (f32[256,2048]{1,0:T(8,128)}, f32[256,4096]{1,0:T(8,128)}, bf16[4096,2048]{1,0:T(8,128)(2,1)}, bf16[256,2048]{1,0:T(8,128)(2,1)}, bf16[4096,256]{1,0:T(8,128)(2,1)}) custom-call(f32[16,16384]{1,0:T(8,128)} %x_ref.1), custom_call_target="tpu_custom_call" | custom-call | tf_op jit(solution)/shard_map/gather_columns/pallas_call | solution.py:409
  92.3 27.7 %gram_blocks.1 = f32[4096,2048]{1,0:T(8,128)} custom-call(bf16[4096,256]{1,0:T(8,128)(2,1)} %get-tuple-element.10.left_ref, f32[256,4096]{1,0:T(8,128)} %get-tuple-element.11.panel_ref, bf16[256,2048]{1,0:T(8,128)(2,1)} %get-tuple-element.12.near_ref, f32[256,2048]{1,0:T(8,128)} %get-tuple-element.13.own_ref, bf16[4096,2048]{1,0:T(8,128)(2,1)} %get-tuple-element.14.cross_ref), custom_call_target="tpu_custom_call" | custom-call | flops 17179869184 | bytes 59768832 | tf_op jit(solution)/shard_map/gram_blocks/pallas_call | solution.py:463

commit v7 on v5

--- a/solution.py
+++ b/solution.py
@@ -10,8 +10,9 @@
 MESH = pl.DeviceIdType.MESH
 CORES = 2
 GROUPS = 8
-LAG = 2
+LAG = 3
 TILE = 512
+ROWS = 256
 VMEM_LIMIT = 56 * 2**20
 
 
@@ -460,16 +461,16 @@
     once = pl.Buffered(1)
     return pl.pallas_call(
         functools.partial(gram_kernel, 0.5 / half),
-        grid=(count // TILE,),
+        grid=(count // ROWS,),
         out_shape=jax.ShapeDtypeStruct((count, width), jnp.float32),
         in_specs=[
-            pl.BlockSpec((TILE, half), lambda i: (i, 0)),
-            pl.BlockSpec((half, TILE), lambda i: (0, i)),
+            pl.BlockSpec((ROWS, half), lambda i: (i, 0)),
+            pl.BlockSpec((half, ROWS), lambda i: (0, i)),
             pl.BlockSpec((half, width), lambda i: (0, 0), pipeline_mode=once),
             pl.BlockSpec((half, width), lambda i: (0, 0), pipeline_mode=once),
-            pl.BlockSpec((TILE, width), lambda i: (i, 0)),
+            pl.BlockSpec((ROWS, width), lambda i: (i, 0)),
         ],
-        out_specs=pl.BlockSpec((TILE, width), lambda i: (i, 0)),
+        out_specs=pl.BlockSpec((ROWS, width), lambda i: (i, 0)),
         scratch_shapes=[pltpu.VMEM((4 * half, width), jnp.bfloat16)],
         compiler_params=pltpu.CompilerParams(vmem_limit_bytes=VMEM_LIMIT),
         cost_estimate=pl.CostEstimate(

time: 120 us -> 125 us (1.042)
  Pallas kernels: 120 us -> 124 us
    pallas_call x1, Pallas kernels: 27.7 us -> 31 us  [gram(): pl.pallas_call(functools.partial(gram_kernel, 0.5 / half), grid=(count //...]
where the time goes in v7:
time: 125 us; the launch traced here: 124 us
  Pallas kernels  124 us (99%)
    pallas_call x1, Pallas kernels, gather(): pl.pallas_call(functools.partial(gather_kernel, n_rows, n_cols, groups),...  93 us
    pallas_call x1, Pallas kernels, gram(): pl.pallas_call(functools.partial(gram_kernel, 0.5 / half), grid=(count //...  31 us

profile of v7, /device:TPU:3, one launch (start us, length us, event | category | flops | bytes accessed | tf_op | source)
XLA Modules:
  0.0 124.1 jit_solution(15612680525132708335)
XLA Ops:
  0.0 93.0 %gather_columns.1 = (f32[256,2048]{1,0:T(8,128)}, f32[256,4096]{1,0:T(8,128)}, bf16[4096,2048]{1,0:T(8,128)(2,1)}, bf16[256,2048]{1,0:T(8,128)(2,1)}, bf16[4096,256]{1,0:T(8,128)(2,1)}) custom-call(f32[16,16384]{1,0:T(8,128)} %x_ref.1), custom_call_target="tpu_custom_call" | custom-call | tf_op jit(solution)/shard_map/gather_columns/pallas_call | solution.py:410
  93.1 31.0 %gram_blocks.1 = f32[4096,2048]{1,0:T(8,128)} custom-call(bf16[4096,256]{1,0:T(8,128)(2,1)} %get-tuple-element.10.left_ref, f32[256,4096]{1,0:T(8,128)} %get-tuple-element.11.panel_ref, bf16[256,2048]{1,0:T(8,128)(2,1)} %get-tuple-element.12.near_ref, f32[256,2048]{1,0:T(8,128)} %get-tuple-element.13.own_ref, bf16[4096,2048]{1,0:T(8,128)(2,1)} %get-tuple-element.14.cross_ref), custom_call_target="tpu_custom_call" | custom-call | flops 17179869184 | bytes 59768832 | tf_op jit(solution)/shard_map/gram_blocks/pallas_call | solution.py:462
